TPU v7x, 32 devices: a whole 2x2x4 slice. The times are simulated.
32 devices in a mesh: pool: 8 (over z, y), blk: 4 (over x, core).
Axes of the slice: x: 2, y: 2, z: 4, core: 2. Of those that a mesh axis runs over, the one named last changes fastest.
Arguments:
- queries: bfloat16 [4096, 4096], P(('pool', 'blk')), may hold values from -7.5 to 7.5
- span_kv: bfloat16 [4096, 1024], P(('pool', 'blk')), may hold values from -6 to 6
- kv_store: bfloat16 [128, 64, 1024], P('pool'), may hold values from -6 to 6
- page_ids: int32 [8, 8], P('pool'), may hold values from 0 to 15
- page_owner: int32 [8, 8], P('pool'), may hold values from 0 to 7, as said below
- prefix_len: int32 [8], P('pool'), may hold values from 320 to 512, as said below
Outputs:
- attended: bfloat16 [4096, 4096], P(('pool', 'blk'))
Inputs may be any that keep to these rules, and one draw needn't show every extreme that they name: `page_owner`: each request's list names 4 owners, each exactly 2 times; one owner is named by every request. `prefix_len`: some request has a prefix of exactly 512 tokens.
All inputs are finite; a program needn't handle non-finite values.
Results may differ from a plain program's by a relative error of at most 0.005.
Values may be sent and summed in bfloat16 or wider, within the bound.
No kernel may reach another device: no remote copies, remote signals or barrier semaphores. Data moves between devices by JAX's collectives and lax.ppermute only.
A program may use at most 128 MiB of HBM per device.

v0:
```python
import functools
import math

import jax
import jax.numpy as jnp
from jax import lax
from jax.experimental import pallas as pl
from jax.experimental.pallas import tpu as pltpu
from jax.sharding import PartitionSpec as P

KVH = 4
DH = 128
GROUP = 8
CAP = 2
COEF = math.log2(math.e) / math.sqrt(DH)
LOW = -1e30
ROWS = 256
LOADS = 4


SMEM = pl.BlockSpec(memory_space=pltpu.SMEM)
VMEM = pl.BlockSpec(memory_space=pltpu.VMEM)
ANY = pl.BlockSpec(memory_space=pl.ANY)


def columns_from(first, count):
    return pl.ds(pl.multiple_of(first * DH, DH), count * DH)


def pick_kernel(tables_ref, store_ref, out_ref, table, own, load_sems, sems):
    pools, _, listed = tables_ref.shape
    stored, rows, _ = own.shape
    blk = lax.axis_index("blk")
    head = lax.rem(blk, KVH)
    at_rows = pl.ds(pl.multiple_of(lax.div(blk, KVH) * rows, rows), rows)
    loads = [pltpu.make_async_copy(tables_ref, table, load_sems.at[0])]
    for kind in range(2):
        for first in range(0, stored, stored // LOADS):
            pages = slice(first, first + stored // LOADS)
            loads.append(
                pltpu.make_async_copy(
                    store_ref.at[pages, at_rows, columns_from(kind * KVH + head, 1)],
                    own.at[pages, :, kind * DH : (kind + 1) * DH],
                    load_sems.at[len(loads)],
                )
            )
    for load in loads:
        load.start()
    for load in loads:
        load.wait()

    def page_copy(request, slot, page):
        return pltpu.make_async_copy(
            own.at[page], out_ref.at[request, slot], sems.at[request, slot]
        )

    def serve(request, carry):
        def visit(entry, state):
            rank, pages = state
            page = table[request, 0, entry]
            hit = page >= 0
            pages = [jnp.where(hit & (rank == slot), page, pages[slot]) for slot in range(CAP)]
            return rank + hit.astype(jnp.int32), pages

        state = (jnp.int32(0), [jnp.int32(0)] * CAP)
        _, pages = lax.fori_loop(0, listed, visit, state, unroll=listed <= 8)
        for slot in range(CAP):
            page_copy(request, slot, pages[slot]).start()
        return carry

    lax.fori_loop(0, pools, serve, 0)

    def finish(request, carry):
        for slot in range(CAP):
            page_copy(request, slot, 0).wait()
        return carry

    lax.fori_loop(0, pools, finish, 0)


def pick_pages(tables, kv_store, rows):
    pools = tables.shape[0]
    return pl.pallas_call(
        pick_kernel,
        in_specs=[ANY, ANY],
        out_specs=ANY,
        out_shape=pltpu.HBM((pools, CAP, rows, 2 * DH), kv_store.dtype),
        scratch_shapes=[
            pltpu.SMEM(tables.shape, jnp.int32),
            pltpu.VMEM((kv_store.shape[0], rows, 2 * DH), kv_store.dtype),
            pltpu.SemaphoreType.DMA((1 + 2 * LOADS,)),
            pltpu.SemaphoreType.DMA((pools, CAP)),
        ],
        name="pick_pages",
    )(in_vmem(tables), in_hbm(kv_store))


def in_hbm(array):
    return pltpu.with_memory_space_constraint(array, pltpu.HBM)


def in_vmem(array):
    return pltpu.with_memory_space_constraint(array, pltpu.VMEM)


def order_kernel(owners_ref, fetched_ref, out_ref):
    for entry in range(out_ref.shape[0]):
        owner = owners_ref[0, entry]
        rank = jnp.int32(0)
        for earlier in range(entry):
            rank += (owners_ref[0, earlier] == owner).astype(jnp.int32)
        out_ref[entry] = fetched_ref[owner, jnp.minimum(rank, CAP - 1)]


def order_pages(owners, fetched):
    listed = owners.shape[1]
    rows = fetched.shape[2]
    return pl.pallas_call(
        order_kernel,
        in_specs=[SMEM, VMEM],
        out_specs=VMEM,
        out_shape=pltpu.VMEM((listed, rows, 2 * DH), fetched.dtype),
        name="order_pages",
    )(owners, in_vmem(fetched))


def scores_of(query_ref, first, count, keys):
    heads = [query_ref[:, (first + j) * DH : (first + j + 1) * DH] for j in range(count)]
    stacked = heads[0] if count == 1 else jnp.concatenate(heads, axis=0)
    return lax.dot_general(
        stacked, keys, (((1,), (1,)), ((), ())), preferred_element_type=jnp.float32
    )


def with_ones(values):
    return jnp.concatenate([values, jnp.ones((values.shape[0], DH), values.dtype)], axis=1)


def span_kernel(masks, parts, rows, limit_ref, query_ref, *refs):
    blocks = len(masks)
    keys_refs, values_refs = refs[:blocks], refs[blocks : 2 * blocks]
    mean_ref, level_ref, copy_ref, bias_ref = refs[2 * blocks :]
    q_rows = query_ref.shape[0]
    count = ROWS // q_rows
    copy_ref[0] = query_ref[...]
    own = lax.axis_index("blk")
    shape = (bias_ref.shape[0], bias_ref.shape[1] // parts)
    index = lax.broadcasted_iota(jnp.int32, shape, 1)
    at_page = lax.div(index, rows) * (parts * rows) + lax.rem(index, rows)
    for step in range(parts):
        position = at_page + lax.rem(lax.div(own, KVH) + step, parts) * rows
        bias_ref[:, step * shape[1] : (step + 1) * shape[1]] = jnp.where(
            position < limit_ref[0], 0.0, LOW
        )
    keys = jnp.concatenate([ref[...] for ref in keys_refs], axis=0)
    values = with_ones(jnp.concatenate([ref[...] for ref in values_refs], axis=0))
    ahead = lax.broadcasted_iota(jnp.int32, (q_rows, q_rows), 0) - lax.broadcasted_iota(
        jnp.int32, (q_rows, q_rows), 1
    )
    bias = [
        jnp.where(ahead >= (jnp.bitwise_xor(own, mask) - own) * q_rows, 0.0, LOW) for mask in masks
    ]
    bias = jnp.concatenate(bias, axis=1)
    bias = jnp.concatenate([bias] * count, axis=0)
    lanes = lax.broadcasted_iota(jnp.int32, (q_rows, DH), 1)
    levels = jnp.zeros((q_rows, DH), jnp.float32)
    for first in range(0, GROUP, count):
        scores = scores_of(query_ref, first, count, keys) + bias
        top = jnp.max(scores, axis=1, keepdims=True)
        weights = jnp.exp2((scores - top) * COEF)
        summed = jnp.dot(
            weights.astype(jnp.bfloat16), values, preferred_element_type=jnp.float32
        )
        total = summed[:, DH:]
        level = top * COEF + jnp.log2(total)
        mean = summed[:, :DH] / total
        for j in range(count):
            at = slice(j * q_rows, (j + 1) * q_rows)
            columns = slice((first + j) * DH, (first + j + 1) * DH)
            mean_ref[0, :, columns] = mean[at].astype(jnp.bfloat16)
            levels = jnp.where(lanes == first + j, level[at], levels)
    level_ref[0] = levels


def attend_span(limit, queries, span, length, parts, rows):
    q_rows = queries.shape[0]
    masks = sorted(span)
    blocks = [span[mask] for mask in masks]
    wide = GROUP * DH

    def head(m):
        return lax.rem(lax.axis_index("blk"), KVH) ^ m

    keys_spec = pl.BlockSpec((q_rows, DH), lambda m: (0, head(m)))
    values_spec = pl.BlockSpec((q_rows, DH), lambda m: (0, KVH + head(m)))
    return pl.pallas_call(
        functools.partial(span_kernel, masks, parts, rows),
        grid=(KVH,),
        in_specs=[SMEM, pl.BlockSpec((q_rows, wide), lambda m: (0, head(m)))]
        + [keys_spec] * len(masks)
        + [values_spec] * len(masks),
        out_specs=[
            pl.BlockSpec((1, q_rows, wide), lambda m: (m, 0, 0)),
            pl.BlockSpec((1, q_rows, DH), lambda m: (m, 0, 0)),
            pl.BlockSpec((1, q_rows, wide), lambda m: (m, 0, 0)),
            pl.BlockSpec((8, length), lambda m: (0, 0)),
        ],
        out_shape=[
            pltpu.VMEM((KVH, q_rows, wide), jnp.bfloat16),
            pltpu.VMEM((KVH, q_rows, DH), jnp.float32),
            pltpu.VMEM((KVH, q_rows, wide), jnp.bfloat16),
            pltpu.VMEM((8, length), jnp.float32),
        ],
        cost_estimate=pl.CostEstimate(
            flops=4 * q_rows * KVH * wide * q_rows * len(masks),
            bytes_accessed=8 * 2**20,
            transcendentals=0,
        ),
        compiler_params=pltpu.CompilerParams(vmem_limit_bytes=48 * 2**20),
        name="attend_span",
    )(limit, in_hbm(queries), *blocks, *blocks)


def prefix_kernel(mask, parts, *refs):
    pieces = refs[:parts]
    query_ref, mean_ref, level_ref, bias_ref, *_, out_ref, done_ref, sems = refs[parts:]
    q_rows = query_ref.shape[1]
    count = ROWS // q_rows
    head = jnp.bitwise_xor(lax.rem(lax.axis_index("blk"), KVH), mask)
    listed, rows, _ = pieces[0].shape
    length = listed * rows
    both = [piece[...].reshape(length, 2 * DH) for piece in pieces]
    both = both[0] if parts == 1 else jnp.concatenate(both, axis=0)
    keys = both[:, :DH]
    values = with_ones(both[:, DH:])
    safe = length * 5 // 8 // DH * DH
    biases = [bias_ref[:1, step * length + safe : (step + 1) * length] for step in range(parts)]
    copies = []
    for first in range(0, GROUP, count):
        raw = scores_of(query_ref.at[mask], first, count, keys)
        scores = []
        for step, bias in enumerate(biases):
            scores.append(raw[:, step * length : step * length + safe])
            scores.append(raw[:, step * length + safe : (step + 1) * length] + bias)
        scores = jnp.concatenate(scores, axis=1)
        heads = [slice((first + j) * DH, (first + j + 1) * DH) for j in range(count)]
        level = jnp.concatenate(
            [
                jnp.broadcast_to(level_ref[mask, :, first + j : first + j + 1], (q_rows, DH))
                for j in range(count)
            ],
            axis=0,
        )
        mean = jnp.concatenate([mean_ref[mask, :, columns] for columns in heads], axis=0)
        top = jnp.maximum(jnp.max(scores, axis=1, keepdims=True) * COEF, level)
        tops = jnp.concatenate([top] * (parts * length // DH), axis=1)
        weights = jnp.exp2(scores * COEF - tops)
        old = jnp.exp2(level - top)
        summed = jnp.dot(
            weights.astype(jnp.bfloat16), values, preferred_element_type=jnp.float32
        )
        result = (summed[:, :DH] + mean.astype(jnp.float32) * old) / (summed[:, DH:] + old)
        for j, columns in enumerate(heads):
            done_ref[:, columns] = result[j * q_rows : (j + 1) * q_rows].astype(jnp.bfloat16)
        copies.append(
            pltpu.make_async_copy(
                done_ref.at[:, first * DH : (first + count) * DH],
                out_ref.at[:, columns_from(head * GROUP + first, count)],
                sems.at[first // count],
            )
        )
        copies[-1].start()
    for copy in copies:
        copy.wait()


def attend_prefix(held, state, partial, mask):
    _, q_rows, wide = state[0].shape
    pieces = [held[at] for at in sorted(held) if at % KVH == mask]
    parts = len(pieces)
    length = parts * pieces[0].shape[0] * pieces[0].shape[1]
    return pl.pallas_call(
        functools.partial(prefix_kernel, mask, parts),
        in_specs=[VMEM] * (parts + len(state)) + [ANY] * len(partial),
        out_specs=ANY,
        out_shape=jax.ShapeDtypeStruct((q_rows, KVH * wide), jnp.bfloat16),
        scratch_shapes=[
            pltpu.VMEM((q_rows, wide), jnp.bfloat16),
            pltpu.SemaphoreType.DMA((GROUP * q_rows // ROWS,)),
        ],
        input_output_aliases={parts + len(state): 0} if partial else {},
        cost_estimate=pl.CostEstimate(
            flops=64 * q_rows * wide * length, bytes_accessed=2**20, transcendentals=0
        ),
        compiler_params=pltpu.CompilerParams(vmem_limit_bytes=48 * 2**20),
        name="attend_prefix",
    )(*pieces, *[in_vmem(array) for array in state], *partial)


def swap(array, blks, mask):
    return lax.ppermute(array, "blk", [(i, i ^ mask) for i in range(blks)])


def per_device(queries, span_kv, kv_store, page_ids, page_owner, prefix_len):
    pools = lax.axis_size("pool")
    blks = lax.axis_size("blk")
    stored, page, _ = kv_store.shape
    parts = blks // KVH
    rows = page // parts

    owner = lax.broadcasted_iota(jnp.int32, (pools, 1, page_ids.shape[1]), 0)
    wanted = jnp.where(page_owner[None] == owner, page_ids[None], -1)
    tables = lax.all_to_all(wanted, "pool", split_axis=0, concat_axis=0, tiled=True)
    picked = pick_pages(tables, kv_store, rows)
    picked, span_kv = lax.optimization_barrier((picked, span_kv))
    fetched = lax.all_to_all(picked, "pool", split_axis=0, concat_axis=0, tiled=True)
    span = {0: span_kv}
    bit = blks // 2
    while bit:
        span.update({mask ^ bit: swap(rows_of, blks, bit) for mask, rows_of in list(span.items())})
        bit //= 2
    length = page_ids.shape[1] * page
    state = attend_span(prefix_len, queries, span, length, parts, rows)
    fetched, *state = lax.optimization_barrier((fetched, *state))
    mean, level, query, bias = state
    state = (query, mean, level, bias)
    held = {0: order_pages(page_owner, fetched)}
    held[1] = swap(held[0], blks, 1)
    bit = blks // 2
    while bit > 1:
        pieces = [(mask, piece) for mask, piece in held.items() if mask % 2 == 0]
        held.update({mask ^ bit: swap(piece, blks, bit) for mask, piece in pieces})
        bit //= 2
    for mask in range(KVH, blks, KVH):
        held[mask ^ 1] = swap(held[mask], blks, 1)
    out = attend_prefix(held, state, [], 0)
    out = attend_prefix(held, state, [out], 1)
    far = {mask: piece for mask, piece in held.items() if mask % KVH == 2}
    out, far = lax.optimization_barrier((out, far))
    far.update({mask ^ 1: swap(piece, blks, 1) for mask, piece in list(far.items())})
    out = attend_prefix(far, state, [out], 2)
    return attend_prefix(far, state, [out], 3)


def solution(mesh):
    in_specs = (
        P(("pool", "blk"), None),
        P(("pool", "blk"), None),
        P("pool", None, None),
        P("pool", None),
        P("pool", None),
        P("pool"),
    )
    out_specs = P(("pool", "blk"), None)
    return jax.shard_map(
        per_device, mesh=mesh, in_specs=in_specs, out_specs=out_specs, check_vma=False
    )
```

profile of v0, /device:TPU:0, one launch (start us, length us, event | category | flops | bytes accessed | tf_op | source)
XLA Modules:
  0.0 46.5 jit_solution(18170760265869488201)
XLA Ops:
  0.0 0.7 %compare_select_fusion = s32[8,1,8]{2,1,0:T(1,128)S(1)} fusion(s32[8]{0:T(128)} %bitcast.3, s32[8]{0:T(128)} %bitcast.2), kind=kLoop, calls=%fused_computation | loop fusion | flops 128 | bytes 320 | tf_op jit(solution)/shard_map/jit(_where)/select_n | solution.py:312
  0.7 13.5 %all_to_all.10.tables_ref = s32[8,1,8]{2,1,0:T(1,128)S(1)} all-to-all(s32[8,1,8]{2,1,0:T(1,128)S(1)} %compare_select_fusion), channel_id=1, replica_groups=mesh['pool'=8,'blk'=4] {'pool'}, dimensions={0} | all-to-all | bytes 512 | tf_op jit(solution)/shard_map/all_to_all | solution.py:313
  14.3 2.1 %pick_pages.1 = bf16[8,2,64,256]{3,2,1,0:T(8,128)(2,1)} custom-call(s32[8,1,8]{2,1,0:T(1,128)S(1)} %all_to_all.10.tables_ref, bf16[16,64,1024]{2,1,0:T(8,128)(2,1)} %store_ref.1), custom_call_target="tpu_custom_call" | custom-call | tf_op jit(solution)/shard_map/pick_pages/pallas_call | solution.py:83
  16.3 3.5 %all-to-all-start.1 = ((bf16[8,2,64,256]{3,2,1,0:T(8,128)(2,1)}), bf16[8,2,64,256]{3,2,1,0:T(8,128)(2,1)S(1)}, u32[]{:S(2)}, u32[]{:S(2)}) async-start(bf16[8,2,64,256]{3,2,1,0:T(8,128)(2,1)} %pick_pages.1), calls=%async_computation.1 | async-start | bytes 1048576 | tf_op jit(solution)/shard_map/all_to_all | solution.py:316
  19.8 0.0 copy-done
  19.9 1.6 %collective-permute-start.1 = (bf16[128,1024]{1,0:T(8,128)(2,1)S(1)}, bf16[128,1024]{1,0:T(8,128)(2,1)S(1)}, u32[]{:S(2)}, u32[]{:S(2)}) collective-permute-start(bf16[128,1024]{1,0:T(8,128)(2,1)S(1)} %copy-done), channel_id=1, source_target_pairs={{0,2},{1,3},{2,0},{3,1},{4,6},{5,7},{6,4},{7,5},{8,10},{9,11},{10,... | collective-permute-start | bytes 786440 | tf_op jit(solution)/shard_map/ppermute | solution.py:301
  21.4 0.0 collective-permute-start
  21.4 5.1 %collective-permute-done.1.refs_2_.refs_6_ = bf16[128,1024]{1,0:T(8,128)(2,1)S(1)} collective-permute-done((bf16[128,1024]{1,0:T(8,128)(2,1)S(1)}, bf16[128,1024]{1,0:T(8,128)(2,1)S(1)}, u32[]{:S(2)}, u32[]{:S(2)}) %collective-permute-start.1) | collective-permute-done | bytes 262176 | tf_op jit(solution)/shard_map/ppermute | solution.py:301
  26.5 0.0 collective-permute-start.2
  27.2 0.0 collective-permute-done.refs_1_.refs_5_
  27.2 0.9 %collective-permute-done.2.refs_3_.refs_7_ = bf16[128,1024]{1,0:T(8,128)(2,1)S(1)} collective-permute-done((bf16[128,1024]{1,0:T(8,128)(2,1)S(1)}, bf16[128,1024]{1,0:T(8,128)(2,1)S(1)}, u32[]{:S(2)}, u32[]{:S(2)}) %collective-permute-start.2) | collective-permute-done | bytes 262176 | tf_op jit(solution)/shard_map/ppermute | solution.py:301
  28.1 5.6 %attend_span.1 = (bf16[4,128,1024]{2,1,0:T(8,128)(2,1)S(1)}, f32[4,128,128]{2,1,0:T(8,128)S(1)}, bf16[4,128,1024]{2,1,0:T(8,128)(2,1)S(1)}, f32[8,512]{1,0:T(8,128)S(1)}) custom-call(s32[1]{0:T(128)S(6)} %copy.13.limit_ref, bf16[128,4096]{1,0:T(8,128)(2,1)} %query_ref.1, bf16[128,1024]{1,0:T(8,128)(2,1)S(1)} %copy-done, ...), custom_call_target="tpu_custom_call" | custom-call | flops 1073741824 | bytes 8388608 | tf_op jit(solution)/shard_map/attend_span/pallas_call | solution.py:196
  33.7 0.0 all-to-all-done.1.fetched_ref
  33.7 0.7 %order_pages.1.refs_0_ = bf16[8,64,256]{2,1,0:T(8,128)(2,1)S(1)} custom-call(s32[1,8]{1,0:T(1,128)} %owners_ref.1, bf16[8,2,64,256]{3,2,1,0:T(8,128)(2,1)S(1)} %all-to-all-done.1.fetched_ref), custom_call_target="tpu_custom_call" | custom-call | tf_op jit(solution)/shard_map/order_pages/pallas_call | solution.py:118
  34.4 1.6 %collective-permute-start.4 = (bf16[8,64,256]{2,1,0:T(8,128)(2,1)S(1)}, bf16[8,64,256]{2,1,0:T(8,128)(2,1)S(1)}, u32[]{:S(2)}, u32[]{:S(2)}) collective-permute-start(bf16[8,64,256]{2,1,0:T(8,128)(2,1)S(1)} %order_pages.1.refs_0_), channel_id=1, source_target_pairs={{0,2},{1,3},{2,0},{3,1},{4,6},{5,7},{6,4},{7,5},{8,10},{9,11},{10,... | collective-permute-start | bytes 786440 | tf_op jit(solution)/shard_map/ppermute | solution.py:301
  36.0 0.0 collective-permute-start.3
  36.0 1.8 %attend_prefix.4.refs_5_ = bf16[128,4096]{1,0:T(8,128)(2,1)} custom-call(bf16[8,64,256]{2,1,0:T(8,128)(2,1)S(1)} %order_pages.1.refs_0_, bf16[4,128,1024]{2,1,0:T(8,128)(2,1)S(1)} %get-tuple-element.25.refs_1_, bf16[4,128,1024]{2,1,0:T(8,128)(2,1)S(1)} %get-tuple-element.26.refs_2_, f32[4,128,128]{2,1,0:T(8,128)S(1)} %get-tuple-element.27.refs_3_, ...), custom_call_target="tpu_custom_call" | custom-call | flops 4294967296 | bytes 1048576 | tf_op jit(solution)/shard_map/attend_prefix/pallas_call | solution.py:282
  37.8 0.0 collective-permute-done.3.refs_0_
  37.8 1.8 %attend_prefix.5.refs_5_ = bf16[128,4096]{1,0:T(8,128)(2,1)} custom-call(bf16[8,64,256]{2,1,0:T(8,128)(2,1)S(1)} %collective-permute-done.3.refs_0_, bf16[4,128,1024]{2,1,0:T(8,128)(2,1)S(1)} %get-tuple-element.25.refs_1_, bf16[4,128,1024]{2,1,0:T(8,128)(2,1)S(1)} %get-tuple-element.26.refs_2_, ...), custom_call_target="tpu_custom_call", output_to_operand_aliasing={{}: (5, {})} | custom-call | flops 4294967296 | bytes 1048576 | tf_op jit(solution)/shard_map/attend_prefix/pallas_call | solution.py:282
  39.6 3.2 %collective-permute-done.4.refs_0_ = bf16[8,64,256]{2,1,0:T(8,128)(2,1)S(1)} collective-permute-done((bf16[8,64,256]{2,1,0:T(8,128)(2,1)S(1)}, bf16[8,64,256]{2,1,0:T(8,128)(2,1)S(1)}, u32[]{:S(2)}, u32[]{:S(2)}) %collective-permute-start.4) | collective-permute-done | bytes 262176 | tf_op jit(solution)/shard_map/ppermute | solution.py:301
  42.8 0.0 collective-permute-start.5
  42.8 1.8 %attend_prefix.6.refs_5_ = bf16[128,4096]{1,0:T(8,128)(2,1)} custom-call(bf16[8,64,256]{2,1,0:T(8,128)(2,1)S(1)} %collective-permute-done.4.refs_0_, bf16[4,128,1024]{2,1,0:T(8,128)(2,1)S(1)} %get-tuple-element.25.refs_1_, bf16[4,128,1024]{2,1,0:T(8,128)(2,1)S(1)} %get-tuple-element.26.refs_2_, ...), custom_call_target="tpu_custom_call", output_to_operand_aliasing={{}: (5, {})} | custom-call | flops 4294967296 | bytes 1048576 | tf_op jit(solution)/shard_map/attend_prefix/pallas_call | solution.py:282
  44.6 0.0 collective-permute-done.5.refs_0_
  44.7 1.8 %attend_prefix.7 = bf16[128,4096]{1,0:T(8,128)(2,1)} custom-call(bf16[8,64,256]{2,1,0:T(8,128)(2,1)S(1)} %collective-permute-done.5.refs_0_, bf16[4,128,1024]{2,1,0:T(8,128)(2,1)S(1)} %get-tuple-element.25.refs_1_, bf16[4,128,1024]{2,1,0:T(8,128)(2,1)S(1)} %get-tuple-element.26.refs_2_, ...), custom_call_target="tpu_custom_call", output_to_operand_aliasing={{}: (5, {})} | custom-call | flops 4294967296 | bytes 1048576 | tf_op jit(solution)/shard_map/attend_prefix/pallas_call | solution.py:282
  (1 shorter events, 0.0 us)
Async XLA Ops:
  0.0 19.8 %copy-start = (bf16[128,1024]{1,0:T(8,128)(2,1)S(1)}, bf16[128,1024]{1,0:T(8,128)(2,1)}, u32[]{:S(2)}) copy-start(bf16[128,1024]{1,0:T(8,128)(2,1)} %refs_4_) | copy-start | bytes 786436
  16.3 17.4 %all-to-all-start.1 = ((bf16[8,2,64,256]{3,2,1,0:T(8,128)(2,1)}), bf16[8,2,64,256]{3,2,1,0:T(8,128)(2,1)S(1)}, u32[]{:S(2)}, u32[]{:S(2)}) async-start(bf16[8,2,64,256]{3,2,1,0:T(8,128)(2,1)} %pick_pages.1), calls=%async_computation.1 | async-start | bytes 1048576 | tf_op jit(solution)/shard_map/all_to_all | solution.py:316
  19.9 6.7 %collective-permute-start.1 = (bf16[128,1024]{1,0:T(8,128)(2,1)S(1)}, bf16[128,1024]{1,0:T(8,128)(2,1)S(1)}, u32[]{:S(2)}, u32[]{:S(2)}) collective-permute-start(bf16[128,1024]{1,0:T(8,128)(2,1)S(1)} %copy-done), channel_id=1, source_target_pairs={{0,2},{1,3},{2,0},{3,1},{4,6},{5,7},{6,4},{7,5},{8,10},{9,11},{10,... | collective-permute-start | bytes 786440 | tf_op jit(solution)/shard_map/ppermute | solution.py:301
  21.4 5.8 %collective-permute-start = (bf16[128,1024]{1,0:T(8,128)(2,1)S(1)}, bf16[128,1024]{1,0:T(8,128)(2,1)S(1)}, u32[]{:S(2)}, u32[]{:S(2)}) collective-permute-start(bf16[128,1024]{1,0:T(8,128)(2,1)S(1)} %copy-done), channel_id=1, source_target_pairs={{0,1},{1,0},{2,3},{3,2},{4,5},{5,4},{6,7},{7,6},{8,9},{9,8},{10,11... | collective-permute-start | bytes 786440 | tf_op jit(solution)/shard_map/ppermute | solution.py:301
  26.5 1.5 %collective-permute-start.2 = (bf16[128,1024]{1,0:T(8,128)(2,1)S(1)}, bf16[128,1024]{1,0:T(8,128)(2,1)S(1)}, u32[]{:S(2)}, u32[]{:S(2)}) collective-permute-start(bf16[128,1024]{1,0:T(8,128)(2,1)S(1)} %collective-permute-done.1.refs_2_.refs_6_), channel_id=1, source_target_pairs={{0,1},{1,0},{2,3},{3,2},{4,5},{5,4},{6,7},{7,6},{8,9},{9,8},{10,11... | collective-permute-start | bytes 786440 | tf_op jit(solution)/shard_map/ppermute | solution.py:301
  34.4 8.4 %collective-permute-start.4 = (bf16[8,64,256]{2,1,0:T(8,128)(2,1)S(1)}, bf16[8,64,256]{2,1,0:T(8,128)(2,1)S(1)}, u32[]{:S(2)}, u32[]{:S(2)}) collective-permute-start(bf16[8,64,256]{2,1,0:T(8,128)(2,1)S(1)} %order_pages.1.refs_0_), channel_id=1, source_target_pairs={{0,2},{1,3},{2,0},{3,1},{4,6},{5,7},{6,4},{7,5},{8,10},{9,11},{10,... | collective-permute-start | bytes 786440 | tf_op jit(solution)/shard_map/ppermute | solution.py:301
  36.0 1.8 %collective-permute-start.3 = (bf16[8,64,256]{2,1,0:T(8,128)(2,1)S(1)}, bf16[8,64,256]{2,1,0:T(8,128)(2,1)S(1)}, u32[]{:S(2)}, u32[]{:S(2)}) collective-permute-start(bf16[8,64,256]{2,1,0:T(8,128)(2,1)S(1)} %order_pages.1.refs_0_), channel_id=1, source_target_pairs={{0,1},{1,0},{2,3},{3,2},{4,5},{5,4},{6,7},{7,6},{8,9},{9,8},{10,11... | collective-permute-start | bytes 786440 | tf_op jit(solution)/shard_map/ppermute | solution.py:301
  42.8 1.8 %collective-permute-start.5 = (bf16[8,64,256]{2,1,0:T(8,128)(2,1)S(1)}, bf16[8,64,256]{2,1,0:T(8,128)(2,1)S(1)}, u32[]{:S(2)}, u32[]{:S(2)}) collective-permute-start(bf16[8,64,256]{2,1,0:T(8,128)(2,1)S(1)} %collective-permute-done.4.refs_0_), channel_id=1, source_target_pairs={{0,1},{1,0},{2,3},{3,2},{4,5},{5,4},{6,7},{7,6},{8,9},{9,8},{10,11... | collective-permute-start | bytes 786440 | tf_op jit(solution)/shard_map/ppermute | solution.py:301
where the time goes:
time: 46.8 us; the launch traced here: 46.5 us
  Pallas kernels  15.6 us (33%)
  blocking collectives  13.5 us (29%)
  waiting for transfers between devices  9.23 us (20%)
  starting transfers between devices  6.63 us (14%)
  between operations  0.75 us (2%)
  other arithmetic  0.72 us (2%)
    all_to_all x1, blocking collectives, per_device(): lax.all_to_all(wanted, 'pool', split_axis=0, concat_axis=0, tiled=True)  13.5 us
    ppermute x6, waiting for transfers between devices, swap(): return lax.ppermute(array, 'blk', [(i, i ^ mask) for i in range(blks)])  9.23 us
    pallas_call x4, Pallas kernels, attend_prefix(): pl.pallas_call(functools.partial(prefix_kernel, mask, parts), in_specs=[V...  7.19 us
    pallas_call x1, Pallas kernels, attend_span(): pl.pallas_call(functools.partial(span_kernel, masks, parts, rows), grid=(...  5.62 us
    all_to_all x1, starting transfers between devices, per_device(): lax.all_to_all(picked, 'pool', split_axis=0, concat_axis=0, tiled=True)  3.51 us
    ppermute x6, starting transfers between devices, swap(): return lax.ppermute(array, 'blk', [(i, i ^ mask) for i in range(blks)])  3.12 us
    pallas_call x1, Pallas kernels, pick_pages(): pl.pallas_call(pick_kernel, in_specs=[ANY, ANY], out_specs=ANY, out_shape...  2.07 us
  transfers between devices with their start and end apart: 7, of which 3 were waited for; matrix products, arithmetic and copies ran while one was open for 0% of the time, Pallas kernels for 24%

commit v1 on v0

--- a/solution.py
+++ b/solution.py
@@ -235,9 +235,12 @@
     values = with_ones(both[:, DH:])
     safe = length * 5 // 8 // DH * DH
     biases = [bias_ref[:1, step * length + safe : (step + 1) * length] for step in range(parts)]
-    copies = []
-    for first in range(0, GROUP, count):
-        raw = scores_of(query_ref.at[mask], first, count, keys)
+    starts = range(0, GROUP, count)
+    ahead = scores_of(query_ref.at[mask], 0, count, keys)
+    for first in starts:
+        raw = ahead
+        if first + count < GROUP:
+            ahead = scores_of(query_ref.at[mask], first + count, count, keys)
         scores = []
         for step, bias in enumerate(biases):
             scores.append(raw[:, step * length : step * length + safe])
@@ -262,14 +265,16 @@
         result = (summed[:, :DH] + mean.astype(jnp.float32) * old) / (summed[:, DH:] + old)
         for j, columns in enumerate(heads):
             done_ref[:, columns] = result[j * q_rows : (j + 1) * q_rows].astype(jnp.bfloat16)
-        copies.append(
-            pltpu.make_async_copy(
-                done_ref.at[:, first * DH : (first + count) * DH],
-                out_ref.at[:, columns_from(head * GROUP + first, count)],
-                sems.at[first // count],
-            )
-        )
-        copies[-1].start()
+    copies = [
+        pltpu.make_async_copy(
+            done_ref.at[:, first * DH : (first + count) * DH],
+            out_ref.at[:, columns_from(head * GROUP + first, count)],
+            sems.at[first // count],
+        )
+        for first in starts
+    ]
+    for copy in copies:
+        copy.start()
     for copy in copies:
         copy.wait()
 

time: 46.8 us -> 47 us (level)
  no operation moved by 1% of the time
where the time goes in v1:
time: 47 us; the launch traced here: 46.6 us
  Pallas kernels  15.9 us (34%)
  blocking collectives  13.5 us (29%)
  waiting for transfers between devices  9.1 us (19%)
  starting transfers between devices  6.63 us (14%)
  between operations  0.75 us (2%)
  other arithmetic  0.72 us (2%)
    all_to_all x1, blocking collectives, per_device(): lax.all_to_all(wanted, 'pool', split_axis=0, concat_axis=0, tiled=True)  13.5 us
    ppermute x6, waiting for transfers between devices, swap(): return lax.ppermute(array, 'blk', [(i, i ^ mask) for i in range(blks)])  9.1 us
    pallas_call x4, Pallas kernels, attend_prefix(): pl.pallas_call(functools.partial(prefix_kernel, mask, parts), in_specs=[V...  7.46 us
    pallas_call x1, Pallas kernels, attend_span(): pl.pallas_call(functools.partial(span_kernel, masks, parts, rows), grid=(...  5.62 us
    all_to_all x1, starting transfers between devices, per_device(): lax.all_to_all(picked, 'pool', split_axis=0, concat_axis=0, tiled=True)  3.51 us
    ppermute x6, starting transfers between devices, swap(): return lax.ppermute(array, 'blk', [(i, i ^ mask) for i in range(blks)])  3.12 us
    pallas_call x1, Pallas kernels, pick_pages(): pl.pallas_call(pick_kernel, in_specs=[ANY, ANY], out_specs=ANY, out_shape...  2.07 us
  transfers between devices with their start and end apart: 7, of which 3 were waited for; matrix products, arithmetic and copies ran while one was open for 0% of the time, Pallas kernels for 24%

profile of v1, /device:TPU:0, one launch (start us, length us, event | category | flops | bytes accessed | tf_op | source)
XLA Modules:
  0.0 46.6 jit_solution(2078243657248128349)
XLA Ops:
  0.0 0.7 %compare_select_fusion = s32[8,1,8]{2,1,0:T(1,128)S(1)} fusion(s32[8]{0:T(128)} %bitcast.3, s32[8]{0:T(128)} %bitcast.2), kind=kLoop, calls=%fused_computation | loop fusion | flops 128 | bytes 320 | tf_op jit(solution)/shard_map/jit(_where)/select_n | solution.py:317
  0.7 13.5 %all_to_all.10.tables_ref = s32[8,1,8]{2,1,0:T(1,128)S(1)} all-to-all(s32[8,1,8]{2,1,0:T(1,128)S(1)} %compare_select_fusion), channel_id=1, replica_groups=mesh['pool'=8,'blk'=4] {'pool'}, dimensions={0} | all-to-all | bytes 512 | tf_op jit(solution)/shard_map/all_to_all | solution.py:318
  14.3 2.1 %pick_pages.1 = bf16[8,2,64,256]{3,2,1,0:T(8,128)(2,1)} custom-call(s32[8,1,8]{2,1,0:T(1,128)S(1)} %all_to_all.10.tables_ref, bf16[16,64,1024]{2,1,0:T(8,128)(2,1)} %store_ref.1), custom_call_target="tpu_custom_call" | custom-call | tf_op jit(solution)/shard_map/pick_pages/pallas_call | solution.py:83
  16.3 3.5 %all-to-all-start.1 = ((bf16[8,2,64,256]{3,2,1,0:T(8,128)(2,1)}), bf16[8,2,64,256]{3,2,1,0:T(8,128)(2,1)S(1)}, u32[]{:S(2)}, u32[]{:S(2)}) async-start(bf16[8,2,64,256]{3,2,1,0:T(8,128)(2,1)} %pick_pages.1), calls=%async_computation.1 | async-start | bytes 1048576 | tf_op jit(solution)/shard_map/all_to_all | solution.py:321
  19.8 0.0 copy-done
  19.9 1.6 %collective-permute-start.1 = (bf16[128,1024]{1,0:T(8,128)(2,1)S(1)}, bf16[128,1024]{1,0:T(8,128)(2,1)S(1)}, u32[]{:S(2)}, u32[]{:S(2)}) collective-permute-start(bf16[128,1024]{1,0:T(8,128)(2,1)S(1)} %copy-done), channel_id=1, source_target_pairs={{0,2},{1,3},{2,0},{3,1},{4,6},{5,7},{6,4},{7,5},{8,10},{9,11},{10,... | collective-permute-start | bytes 786440 | tf_op jit(solution)/shard_map/ppermute | solution.py:306
  21.4 0.0 collective-permute-start
  21.4 5.1 %collective-permute-done.1.refs_2_.refs_6_ = bf16[128,1024]{1,0:T(8,128)(2,1)S(1)} collective-permute-done((bf16[128,1024]{1,0:T(8,128)(2,1)S(1)}, bf16[128,1024]{1,0:T(8,128)(2,1)S(1)}, u32[]{:S(2)}, u32[]{:S(2)}) %collective-permute-start.1) | collective-permute-done | bytes 262176 | tf_op jit(solution)/shard_map/ppermute | solution.py:306
  26.5 0.0 collective-permute-start.2
  27.2 0.0 collective-permute-done.refs_1_.refs_5_
  27.2 0.9 %collective-permute-done.2.refs_3_.refs_7_ = bf16[128,1024]{1,0:T(8,128)(2,1)S(1)} collective-permute-done((bf16[128,1024]{1,0:T(8,128)(2,1)S(1)}, bf16[128,1024]{1,0:T(8,128)(2,1)S(1)}, u32[]{:S(2)}, u32[]{:S(2)}) %collective-permute-start.2) | collective-permute-done | bytes 262176 | tf_op jit(solution)/shard_map/ppermute | solution.py:306
  28.1 5.6 %attend_span.1 = (bf16[4,128,1024]{2,1,0:T(8,128)(2,1)S(1)}, f32[4,128,128]{2,1,0:T(8,128)S(1)}, bf16[4,128,1024]{2,1,0:T(8,128)(2,1)S(1)}, f32[8,512]{1,0:T(8,128)S(1)}) custom-call(s32[1]{0:T(128)S(6)} %copy.13.limit_ref, bf16[128,4096]{1,0:T(8,128)(2,1)} %query_ref.1, bf16[128,1024]{1,0:T(8,128)(2,1)S(1)} %copy-done, ...), custom_call_target="tpu_custom_call" | custom-call | flops 1073741824 | bytes 8388608 | tf_op jit(solution)/shard_map/attend_span/pallas_call | solution.py:196
  33.7 0.0 all-to-all-done.1.fetched_ref
  33.7 0.7 %order_pages.1.refs_0_ = bf16[8,64,256]{2,1,0:T(8,128)(2,1)S(1)} custom-call(s32[1,8]{1,0:T(1,128)} %owners_ref.1, bf16[8,2,64,256]{3,2,1,0:T(8,128)(2,1)S(1)} %all-to-all-done.1.fetched_ref), custom_call_target="tpu_custom_call" | custom-call | tf_op jit(solution)/shard_map/order_pages/pallas_call | solution.py:118
  34.4 1.6 %collective-permute-start.4 = (bf16[8,64,256]{2,1,0:T(8,128)(2,1)S(1)}, bf16[8,64,256]{2,1,0:T(8,128)(2,1)S(1)}, u32[]{:S(2)}, u32[]{:S(2)}) collective-permute-start(bf16[8,64,256]{2,1,0:T(8,128)(2,1)S(1)} %order_pages.1.refs_0_), channel_id=1, source_target_pairs={{0,2},{1,3},{2,0},{3,1},{4,6},{5,7},{6,4},{7,5},{8,10},{9,11},{10,... | collective-permute-start | bytes 786440 | tf_op jit(solution)/shard_map/ppermute | solution.py:306
  36.0 0.0 collective-permute-start.3
  36.0 1.9 %attend_prefix.4.refs_5_ = bf16[128,4096]{1,0:T(8,128)(2,1)} custom-call(bf16[8,64,256]{2,1,0:T(8,128)(2,1)S(1)} %order_pages.1.refs_0_, bf16[4,128,1024]{2,1,0:T(8,128)(2,1)S(1)} %get-tuple-element.25.refs_1_, bf16[4,128,1024]{2,1,0:T(8,128)(2,1)S(1)} %get-tuple-element.26.refs_2_, f32[4,128,128]{2,1,0:T(8,128)S(1)} %get-tuple-element.27.refs_3_, ...), custom_call_target="tpu_custom_call" | custom-call | flops 4294967296 | bytes 1048576 | tf_op jit(solution)/shard_map/attend_prefix/pallas_call | solution.py:287
  37.9 0.0 collective-permute-done.3.refs_0_
  37.9 1.9 %attend_prefix.5.refs_5_ = bf16[128,4096]{1,0:T(8,128)(2,1)} custom-call(bf16[8,64,256]{2,1,0:T(8,128)(2,1)S(1)} %collective-permute-done.3.refs_0_, bf16[4,128,1024]{2,1,0:T(8,128)(2,1)S(1)} %get-tuple-element.25.refs_1_, bf16[4,128,1024]{2,1,0:T(8,128)(2,1)S(1)} %get-tuple-element.26.refs_2_, ...), custom_call_target="tpu_custom_call", output_to_operand_aliasing={{}: (5, {})} | custom-call | flops 4294967296 | bytes 1048576 | tf_op jit(solution)/shard_map/attend_prefix/pallas_call | solution.py:287
  39.7 3.1 %collective-permute-done.4.refs_0_ = bf16[8,64,256]{2,1,0:T(8,128)(2,1)S(1)} collective-permute-done((bf16[8,64,256]{2,1,0:T(8,128)(2,1)S(1)}, bf16[8,64,256]{2,1,0:T(8,128)(2,1)S(1)}, u32[]{:S(2)}, u32[]{:S(2)}) %collective-permute-start.4) | collective-permute-done | bytes 262176 | tf_op jit(solution)/shard_map/ppermute | solution.py:306
  42.8 0.0 collective-permute-start.5
  42.8 1.9 %attend_prefix.6.refs_5_ = bf16[128,4096]{1,0:T(8,128)(2,1)} custom-call(bf16[8,64,256]{2,1,0:T(8,128)(2,1)S(1)} %collective-permute-done.4.refs_0_, bf16[4,128,1024]{2,1,0:T(8,128)(2,1)S(1)} %get-tuple-element.25.refs_1_, bf16[4,128,1024]{2,1,0:T(8,128)(2,1)S(1)} %get-tuple-element.26.refs_2_, ...), custom_call_target="tpu_custom_call", output_to_operand_aliasing={{}: (5, {})} | custom-call | flops 4294967296 | bytes 1048576 | tf_op jit(solution)/shard_map/attend_prefix/pallas_call | solution.py:287
  44.7 0.0 collective-permute-done.5.refs_0_
  44.7 1.9 %attend_prefix.7 = bf16[128,4096]{1,0:T(8,128)(2,1)} custom-call(bf16[8,64,256]{2,1,0:T(8,128)(2,1)S(1)} %collective-permute-done.5.refs_0_, bf16[4,128,1024]{2,1,0:T(8,128)(2,1)S(1)} %get-tuple-element.25.refs_1_, bf16[4,128,1024]{2,1,0:T(8,128)(2,1)S(1)} %get-tuple-element.26.refs_2_, ...), custom_call_target="tpu_custom_call", output_to_operand_aliasing={{}: (5, {})} | custom-call | flops 4294967296 | bytes 1048576 | tf_op jit(solution)/shard_map/attend_prefix/pallas_call | solution.py:287
  (1 shorter events, 0.0 us)
Async XLA Ops:
  0.0 19.8 %copy-start = (bf16[128,1024]{1,0:T(8,128)(2,1)S(1)}, bf16[128,1024]{1,0:T(8,128)(2,1)}, u32[]{:S(2)}) copy-start(bf16[128,1024]{1,0:T(8,128)(2,1)} %refs_4_) | copy-start | bytes 786436
  16.3 17.4 %all-to-all-start.1 = ((bf16[8,2,64,256]{3,2,1,0:T(8,128)(2,1)}), bf16[8,2,64,256]{3,2,1,0:T(8,128)(2,1)S(1)}, u32[]{:S(2)}, u32[]{:S(2)}) async-start(bf16[8,2,64,256]{3,2,1,0:T(8,128)(2,1)} %pick_pages.1), calls=%async_computation.1 | async-start | bytes 1048576 | tf_op jit(solution)/shard_map/all_to_all | solution.py:321
  19.9 6.7 %collective-permute-start.1 = (bf16[128,1024]{1,0:T(8,128)(2,1)S(1)}, bf16[128,1024]{1,0:T(8,128)(2,1)S(1)}, u32[]{:S(2)}, u32[]{:S(2)}) collective-permute-start(bf16[128,1024]{1,0:T(8,128)(2,1)S(1)} %copy-done), channel_id=1, source_target_pairs={{0,2},{1,3},{2,0},{3,1},{4,6},{5,7},{6,4},{7,5},{8,10},{9,11},{10,... | collective-permute-start | bytes 786440 | tf_op jit(solution)/shard_map/ppermute | solution.py:306
  21.4 5.8 %collective-permute-start = (bf16[128,1024]{1,0:T(8,128)(2,1)S(1)}, bf16[128,1024]{1,0:T(8,128)(2,1)S(1)}, u32[]{:S(2)}, u32[]{:S(2)}) collective-permute-start(bf16[128,1024]{1,0:T(8,128)(2,1)S(1)} %copy-done), channel_id=1, source_target_pairs={{0,1},{1,0},{2,3},{3,2},{4,5},{5,4},{6,7},{7,6},{8,9},{9,8},{10,11... | collective-permute-start | bytes 786440 | tf_op jit(solution)/shard_map/ppermute | solution.py:306
  26.5 1.5 %collective-permute-start.2 = (bf16[128,1024]{1,0:T(8,128)(2,1)S(1)}, bf16[128,1024]{1,0:T(8,128)(2,1)S(1)}, u32[]{:S(2)}, u32[]{:S(2)}) collective-permute-start(bf16[128,1024]{1,0:T(8,128)(2,1)S(1)} %collective-permute-done.1.refs_2_.refs_6_), channel_id=1, source_target_pairs={{0,1},{1,0},{2,3},{3,2},{4,5},{5,4},{6,7},{7,6},{8,9},{9,8},{10,11... | collective-permute-start | bytes 786440 | tf_op jit(solution)/shard_map/ppermute | solution.py:306
  34.4 8.4 %collective-permute-start.4 = (bf16[8,64,256]{2,1,0:T(8,128)(2,1)S(1)}, bf16[8,64,256]{2,1,0:T(8,128)(2,1)S(1)}, u32[]{:S(2)}, u32[]{:S(2)}) collective-permute-start(bf16[8,64,256]{2,1,0:T(8,128)(2,1)S(1)} %order_pages.1.refs_0_), channel_id=1, source_target_pairs={{0,2},{1,3},{2,0},{3,1},{4,6},{5,7},{6,4},{7,5},{8,10},{9,11},{10,... | collective-permute-start | bytes 786440 | tf_op jit(solution)/shard_map/ppermute | solution.py:306
  36.0 1.9 %collective-permute-start.3 = (bf16[8,64,256]{2,1,0:T(8,128)(2,1)S(1)}, bf16[8,64,256]{2,1,0:T(8,128)(2,1)S(1)}, u32[]{:S(2)}, u32[]{:S(2)}) collective-permute-start(bf16[8,64,256]{2,1,0:T(8,128)(2,1)S(1)} %order_pages.1.refs_0_), channel_id=1, source_target_pairs={{0,1},{1,0},{2,3},{3,2},{4,5},{5,4},{6,7},{7,6},{8,9},{9,8},{10,11... | collective-permute-start | bytes 786440 | tf_op jit(solution)/shard_map/ppermute | solution.py:306
  42.8 1.9 %collective-permute-start.5 = (bf16[8,64,256]{2,1,0:T(8,128)(2,1)S(1)}, bf16[8,64,256]{2,1,0:T(8,128)(2,1)S(1)}, u32[]{:S(2)}, u32[]{:S(2)}) collective-permute-start(bf16[8,64,256]{2,1,0:T(8,128)(2,1)S(1)} %collective-permute-done.4.refs_0_), channel_id=1, source_target_pairs={{0,1},{1,0},{2,3},{3,2},{4,5},{5,4},{6,7},{7,6},{8,9},{9,8},{10,11... | collective-permute-start | bytes 786440 | tf_op jit(solution)/shard_map/ppermute | solution.py:306
